TPU v7x, 1024 devices: a whole 8x8x8 slice. The times are simulated.
1024 devices in a mesh: seq: 64 (over y, z), dp: 16 (over x, core).
Axes of the slice: x: 8, y: 8, z: 8, core: 2. Of those that a mesh axis runs over, the one named last changes fastest.
Arguments:
- queries: bfloat16 [8192, 8192], P('seq', 'dp'), may hold values from -6 to 6
- keys: bfloat16 [8192, 8192], P('seq', 'dp'), may hold values from -0.59765625 to 0.59765625
- values: bfloat16 [8192, 8192], P('seq', 'dp'), may hold values from -6 to 6
- output_gradient: bfloat16 [8192, 8192], P('seq', 'dp'), may hold values from -6 to 6
- log_decay: float32 [64, 8192], P('dp', 'seq'), may hold values from -1 to 0, as said below
- gain: float32 [8192], P('dp'), may hold values from 0.1 to 1.9
Outputs:
- query_grad: bfloat16 [8192, 8192], P('seq', 'dp')
- key_grad: bfloat16 [8192, 8192], P('seq', 'dp')
- value_grad: bfloat16 [8192, 8192], P('seq', 'dp')
- gain_grad: float32 [8192], P('dp')
Inputs may be any that keep to these rules, and one draw needn't show every extreme that they name: `log_decay`: negative at every token and head.
All inputs are finite; a program needn't handle non-finite values.
Results may differ from a plain program's by a relative error of at most 0.005.
Values sent between devices are 32-bit elements; how exact they have to be, the bound alone decides.
A program may use at most 128 MiB of HBM per device.

v0:
```python
import jax
import jax.numpy as jnp
from jax import lax
from jax.sharding import PartitionSpec as P

epsilon = 1e-05
highest = lax.Precision.HIGHEST


def entering(value, axis, join, neutral, backward):
    count, mine = (lax.axis_size(axis), lax.axis_index(axis))
    pieces = jax.tree.map(lambda part: lax.all_gather(part, axis), value)
    if backward:
        pieces = jax.tree.map(lambda part: part[::-1], pieces)
        mine = count - 1 - mine
    subtotal = jax.tree.map(
        lambda part, zero: jnp.full_like(part, 0) + jnp.asarray(zero, part.dtype), value, neutral
    )

    def turn(position, subtotal):
        longer = join(subtotal, jax.tree.map(lambda part: part[position], pieces))
        return jax.tree.map(lambda new, old: jnp.where(position < mine, new, old), longer, subtotal)

    return lax.fori_loop(0, count - 1, turn, subtotal)


def forward_combine(earlier, later):
    return (earlier[0] * later[0], later[0][:, None] * earlier[1] + later[1])


def backward_combine(earlier, later):
    return (earlier[0] * later[0], later[1] + later[0][:, None] * earlier[1])


def on_device(queries, keys, values, output_gradient, log_decay, gain):
    tok_count = queries.shape[0]
    width = queries.shape[1]
    heads = log_decay.shape[0]
    head_dim = width // heads
    full_width = width * lax.axis_size("dp")
    query_rows = queries.reshape(tok_count, heads, head_dim)
    key_rows = keys.reshape(tok_count, heads, head_dim)
    value_rows = values.reshape(tok_count, heads, head_dim)
    cumulative = jnp.cumsum(log_decay, axis=1)
    last = cumulative[:, -1]
    row_index = lax.broadcasted_iota(jnp.int32, (tok_count, tok_count), 0)
    col_index = lax.broadcasted_iota(jnp.int32, (tok_count, tok_count), 1)
    causal_mask = row_index >= col_index
    weights = jnp.where(
        causal_mask[None],
        jnp.exp(jnp.minimum(cumulative[:, :, None] - cumulative[:, None, :], 0.0)),
        0.0,
    )
    tail_t = jnp.exp(last[:, None] - cumulative).T[:, :, None]
    lead_t = jnp.exp(cumulative).T[:, :, None]
    total_decay = jnp.exp(last)
    key_f = key_rows.astype(jnp.float32)
    value_f = value_rows.astype(jnp.float32)
    query_f = query_rows.astype(jnp.float32)
    local_state = jnp.einsum("thd,the->hde", key_f * tail_t, value_f, precision=highest)
    local_state = local_state.reshape(heads, head_dim * head_dim)
    identity = (
        jnp.ones((heads,), jnp.float32),
        jnp.zeros((heads, head_dim * head_dim), jnp.float32),
    )
    incoming = entering((total_decay, local_state), "seq", forward_combine, identity, False)[1]
    incoming = incoming.reshape(heads, head_dim, head_dim)
    similarity_matrix = jnp.einsum(
        "thd,shd->hts", query_rows, key_rows, preferred_element_type=jnp.float32
    )
    mixed = (similarity_matrix * weights).astype(jnp.bfloat16)
    inner = jnp.einsum("hts,shd->thd", mixed, value_rows, preferred_element_type=jnp.float32)
    outer = jnp.einsum("thd,hde->the", query_f, incoming, precision=highest) * lead_t
    attn = (inner + outer).reshape(tok_count, width)
    grad_f = output_gradient.astype(jnp.float32)
    multiplied_entries = grad_f * gain
    square_sum, cross_sum = lax.psum(
        (jnp.sum(attn * attn, axis=-1), jnp.sum(multiplied_entries * attn, axis=-1)), "dp"
    )
    inv_rms = lax.rsqrt(square_sum / full_width + epsilon)[:, None]
    normed = attn * inv_rms
    cross_mean = inv_rms * (cross_sum / full_width)[:, None]
    d_attn = (inv_rms * (multiplied_entries - normed * cross_mean)).astype(jnp.bfloat16)
    gain_part = jnp.sum(grad_f * normed, axis=0)
    d_attn_rows = d_attn.reshape(tok_count, heads, head_dim)
    d_attn_f = d_attn_rows.astype(jnp.float32)
    local_back = jnp.einsum("thd,the->hde", query_f * lead_t, d_attn_f, precision=highest)
    local_back = local_back.reshape(heads, head_dim * head_dim)
    later = entering((total_decay, local_back), "seq", backward_combine, identity, True)[1]
    later = later.reshape(heads, head_dim, head_dim)
    dprod = jnp.einsum("thd,shd->hts", d_attn_rows, value_rows, preferred_element_type=jnp.float32)
    graded = (dprod * weights).astype(jnp.bfloat16)
    query_grad = jnp.einsum("hts,shd->thd", graded, key_rows, preferred_element_type=jnp.float32)
    query_grad = (
        query_grad + jnp.einsum("the,hde->thd", d_attn_f, incoming, precision=highest) * lead_t
    )
    key_grad = jnp.einsum("hts,thd->shd", graded, query_rows, preferred_element_type=jnp.float32)
    key_grad = key_grad + jnp.einsum("the,hde->thd", value_f, later, precision=highest) * tail_t
    value_grad = jnp.einsum("hts,thd->shd", mixed, d_attn_rows, preferred_element_type=jnp.float32)
    value_grad = value_grad + jnp.einsum("thd,hde->the", key_f, later, precision=highest) * tail_t
    gain_grad = lax.psum(gain_part, "seq")
    return (
        query_grad.reshape(tok_count, width).astype(jnp.bfloat16),
        key_grad.reshape(tok_count, width).astype(jnp.bfloat16),
        value_grad.reshape(tok_count, width).astype(jnp.bfloat16),
        gain_grad,
    )


def solution(mesh):
    return jax.shard_map(
        on_device,
        mesh=mesh,
        in_specs=(
            P("seq", "dp"),
            P("seq", "dp"),
            P("seq", "dp"),
            P("seq", "dp"),
            P("dp", "seq"),
            P("dp"),
        ),
        out_specs=(P("seq", "dp"), P("seq", "dp"), P("seq", "dp"), P("dp")),
        check_vma=False,
    )
```

profile of v0, /device:TPU:1, one launch (start us, length us, event | category | flops | bytes accessed | tf_op | source)
XLA Modules:
  0.0 538.1 jit_solution(16195881729726146535)
XLA Ops:
  10.7 1.3 dynamic-slice
  12.9 131.4 %all-reduce = f32[256]{0:T(256)S(1)} all-reduce(f32[256]{0:T(256)S(1)} %dynamic-update-slice), channel_id=2, replica_groups=mesh['seq'=64,'dp'=16] {'seq'}, use_global_device_ids=true, to_apply=%add | all-reduce | flops 256 | bytes 2048
  145.9 27.4 %all-gather.4.cloned.1.call-done = f32[64,4,16384]{2,1,0:T(4,128)} async-done(((f32[1,4,16384]{2,1,0:T(4,128)}), f32[64,4,16384]{2,1,0:T(4,128)}) %all-gather.4.cloned.1.call-update) | async-done | bytes 16777232 | tf_op jit(solution)/shard_map/all_gather | solution.py:12
  173.3 72.2 %while.28 = (s32[]{:T(128)}, f32[4,16384]{1,0:T(4,128)S(1)}, s32[]{:T(128)}, f32[64,4]{1,0:T(8,128)S(1)}, f32[64,4,16384]{2,1,0:T(4,128)}, /*index=5*/s32[]{:T(128)}, s32[]{:T(128)}) while((s32[]{:T(128)}, f32[4,16384]{1,0:T(4,128)S(1)}, s32[]{:T(128)}, f32[64,4]{1,0:T(8,128)S(1)}, f32[64,4,16384]{2,1,0:T(4,128)}, ...), condition=%wide.region_2.3_spmd.clone, body=%wide.region_1.2_spmd.clone.sunk | while | flops 262148 | bytes 786585 | solution.py:24
  245.9 24.9 %psum.21 = f32[128]{0:T(128)S(1)} all-reduce(f32[128]{0:T(128)S(1)} %get-tuple-element.268), channel_id=1, replica_groups=mesh['seq'=64,'dp'=16] {'dp'}, use_global_device_ids=true, to_apply=%region_4.5 | all-reduce | flops 128 | bytes 1024 | tf_op jit(solution)/shard_map/psum | solution.py:77
  272.1 24.3 %psum.22 = f32[128]{0:T(128)S(1)} all-reduce(f32[128]{0:T(128)S(1)} %get-tuple-element.243), channel_id=1, replica_groups=mesh['seq'=64,'dp'=16] {'dp'}, use_global_device_ids=true, to_apply=%region_6.7 | all-reduce | flops 128 | bytes 1024 | tf_op jit(solution)/shard_map/psum | solution.py:77
  300.3 115.5 %psum.23 = f32[512]{0:T(512)} all-reduce(f32[512]{0:T(512)S(1)} %get-tuple-element.242), channel_id=1, replica_groups=mesh['seq'=64,'dp'=16] {'seq'}, use_global_device_ids=true, to_apply=%region_10.11 | all-reduce | flops 512 | bytes 4096 | tf_op jit(solution)/shard_map/psum | solution.py:101
  416.1 26.7 %all-gather.6.cloned.1.call-done = f32[64,4,16384]{2,1,0:T(4,128)} async-done(((f32[1,4,16384]{2,1,0:T(4,128)}), f32[64,4,16384]{2,1,0:T(4,128)}) %all-gather.6.cloned.1.call-update) | async-done | bytes 16777232 | tf_op jit(solution)/shard_map/all_gather | solution.py:12
  442.8 13.8 %rev.6 = f32[64,4,16384]{2,1,0:T(4,128)} reverse(f32[64,4,16384]{2,1,0:T(4,128)} %all-gather.6.cloned.1.call-done), dimensions={0} | reverse | bytes 33554432 | tf_op jit(solution)/shard_map/rev | solution.py:14
  456.6 72.3 %while.29 = (s32[]{:T(128)}, f32[4,16384]{1,0:T(4,128)S(1)}, s32[]{:T(128)}, f32[64,4,16384]{2,1,0:T(4,128)}, f32[64,4]{1,0:T(8,128)S(1)}, /*index=5*/s32[]{:T(128)}, s32[]{:T(128)}) while((s32[]{:T(128)}, f32[4,16384]{1,0:T(4,128)S(1)}, s32[]{:T(128)}, f32[64,4,16384]{2,1,0:T(4,128)}, f32[64,4]{1,0:T(8,128)S(1)}, ...), condition=%wide.region_8.9_spmd.clone, body=%wide.region_7.8_spmd.clone.sunk | while | flops 262148 | bytes 786585 | solution.py:24
  457.8 1.1 fusion.66
  458.9 1.1 fusion.66
  460.1 1.1 fusion.66
  461.2 1.1 fusion.66
  462.4 1.1 fusion.66
  463.5 1.1 fusion.66
  464.7 1.1 fusion.66
  465.8 1.1 fusion.66
  467.0 1.1 fusion.66
  468.1 1.1 fusion.66
  469.3 1.1 fusion.66
  470.4 1.1 fusion.66
  471.6 1.1 fusion.66
  472.7 1.1 fusion.66
  473.8 1.1 fusion.66
  475.0 1.1 fusion.66
  476.1 1.1 fusion.66
  477.3 1.1 fusion.66
  478.4 1.1 fusion.66
  479.6 1.1 fusion.66
  480.7 1.1 fusion.66
  481.9 1.1 fusion.66
  483.0 1.1 fusion.66
  484.2 1.1 fusion.66
  485.3 1.1 fusion.66
  486.5 1.1 fusion.66
  487.6 1.1 fusion.66
  488.8 1.1 fusion.66
  489.9 1.1 fusion.66
  491.1 1.1 fusion.66
  492.2 1.1 fusion.66
  493.4 1.1 fusion.66
  494.5 1.1 fusion.66
  495.7 1.1 fusion.66
  496.8 1.1 fusion.66
  498.0 1.1 fusion.66
  499.1 1.1 fusion.66
  500.2 1.1 fusion.66
  501.4 1.1 fusion.66
  502.5 1.1 fusion.66
  503.7 1.1 fusion.66
  504.8 1.1 fusion.66
  506.0 1.1 fusion.66
  507.1 1.1 fusion.66
  508.3 1.1 fusion.66
  509.4 1.1 fusion.66
  510.6 1.1 fusion.66
  511.7 1.1 fusion.66
  512.9 1.1 fusion.66
  514.0 1.1 fusion.66
  515.2 1.1 fusion.66
  519.8 1.1 fusion.66
  524.4 1.1 fusion.66
  527.8 1.1 fusion.66
  (239 shorter events, 94.5 us)
Async XLA Ops:
  7.2 2.4 copy-start
  7.2 166.1 %all-gather.4.cloned.1.call-start = ((), (), s32[]{:S(2)}) async-start(), calls=%async_computation | async-start | bytes 17039360 | tf_op jit(solution)/shard_map/all_gather | solution.py:12
  10.7 432.2 %all-gather.6.cloned.1.call-start = ((), (), s32[]{:S(2)}) async-start(), calls=%async_computation.1 | async-start | bytes 17039360 | tf_op jit(solution)/shard_map/all_gather | solution.py:12
Sparse Core Ops, SparseCore 0:
  12.2 161.0 all-gather.3
  298.9 143.9 all-gather.5
where the time goes:
time: 542 us; the launch traced here: 538 us
  blocking collectives  296 us (55%)
  other arithmetic  143 us (26%)
  waiting for transfers between devices  54.1 us (10%)
  local copies, waits for them, and re-layouts  23 us (4%)
  between operations  14.9 us (3%)
    select_n x126, other arithmetic, turn(): jnp.where(position < mine, new, old)  140 us
    unnamed x1, blocking collectives  131 us
    psum x1, blocking collectives, on_device(): gain_grad = lax.psum(gain_part, 'seq')  115 us
    all_gather x2, waiting for transfers between devices, entering(): pieces = jax.tree.map(lambda part: lax.all_gather(part, axis), value)  54.1 us
    psum x2, blocking collectives, on_device(): lax.psum((jnp.sum(attn * attn, axis=-1), jnp.sum(multiplied_entries * att...  49.2 us
    rev x2, local copies, waits for them, and re-layouts, entering(): pieces = jax.tree.map(lambda part: part[::-1], pieces)  13.8 us
  transfers between devices with their start and end apart: 2, of which 2 were waited for; matrix products, arithmetic and copies ran while one was open for 1% of the time, Pallas kernels for 0%

commit v1 on v0

v1 whole, which is shorter than its diff:
```python
import functools

import jax
import jax.numpy as jnp
from jax import lax
from jax.experimental import pallas as pl
from jax.experimental.pallas import tpu as pltpu
from jax.sharding import PartitionSpec as P

MESH = pl.DeviceIdType.MESH
EPS = 1e-05
F32, BF16 = jnp.float32, jnp.bfloat16
HIGHEST = lax.Precision.HIGHEST
H, D, T = 4, 128, 128
SIDE, N_SEQ, N_DP = 8, 64, 16


def _ring(step):
    return min(step, SIDE - step)


STEPS = sorted(
    ((dy, dz) for dy in range(SIDE) for dz in range(SIDE) if dy or dz),
    key=lambda s: -(_ring(s[0]) + _ring(s[1])),
)
DP_STEPS = sorted(range(1, N_DP), key=lambda s: -_ring(s // 2))


def dot(a, b, ca=1, cb=0, precision=None):
    return lax.dot_general(
        a, b, (((ca,), (cb,)), ((), ())), precision=precision, preferred_element_type=F32
    )


def split(x):
    hi = x.astype(BF16)
    return hi, (x - hi.astype(F32)).astype(BF16)


def dot_fine_left(a, b, ca=1, cb=0):
    hi, lo = split(a)
    return dot(hi, b, ca, cb) + dot(lo, b, ca, cb)


def dot_fine_right(a, b, ca=1, cb=0):
    hi, lo = split(b)
    return dot(a, hi, ca, cb) + dot(a, lo, ca, cb)


def kernel(
    q_ref, k_ref, v_ref, g_ref, ld_ref, gain_ref,
    dq_ref, dk_ref, dv_ref, dg_ref,
    snd1, rcv1, out1, inc, snd2, rcv2, out2, lat, dec_snd, dec,
    stat_snd, stat, gz_snd, gz, gy_snd, gy,
    qt, weights, mixed, attn, d_attn, kg, vg,
    send_sems, recv_sems,
):
    me = lax.axis_index("seq")
    mine = lax.axis_index("dp")
    y, z = lax.div(me, SIDE), lax.rem(me, SIDE)
    rows = [lax.rem(y + k, SIDE) * SIDE for k in range(SIDE)]
    cols = [lax.rem(z + k, SIDE) for k in range(SIDE)]
    peers = [rows[dy] + cols[dz] for dy, dz in STEPS]
    partners = [lax.rem(mine + k, N_DP) for k in DP_STEPS]

    barrier = pltpu.get_barrier_semaphore()
    for p in peers:
        pl.semaphore_signal(barrier, inc=1, device_id={"seq": p}, device_id_type=MESH)
    for p in partners:
        pl.semaphore_signal(barrier, inc=1, device_id={"dp": p}, device_id_type=MESH)

    def send(src, dst, at, where):
        pltpu.make_async_remote_copy(
            src_ref=src, dst_ref=dst, send_sem=send_sems.at[at], recv_sem=recv_sems.at[at],
            device_id=where, device_id_type=MESH,
        ).start()

    def arrived(buffer, count, at, sems=recv_sems):
        part = buffer.at[pl.ds(0, count)]
        pltpu.make_async_copy(part, part, sems.at[at]).wait()

    def exchange(src, dst, at):
        for p in peers:
            send(src.at[p], dst.at[me], at, {"seq": p})
        dst[me] = src[me]

    row_i = lax.broadcasted_iota(jnp.int32, (T, T), 0)
    col_i = lax.broadcasted_iota(jnp.int32, (T, T), 1)
    lower = row_i >= col_i
    log_decay = ld_ref[...]
    cum_row = dot(log_decay, jnp.where(row_i <= col_i, 1.0, 0.0), precision=HIGHEST)
    cum_col = dot(jnp.where(lower, 1.0, 0.0), log_decay, 1, 1, precision=HIGHEST)
    last_row = cum_row[:, T - 1:]
    tail_row = jnp.exp(last_row - cum_row)
    lead_row = jnp.exp(cum_row)
    tail_col = jnp.exp(cum_col[T - 1:, :] - cum_col)
    lead_col = jnp.exp(cum_col)
    total = jnp.broadcast_to(jnp.exp(last_row), (H, T))

    def head(ref, h):
        return ref[:, h * D:(h + 1) * D]

    kt = []
    for h in range(H):
        dec_snd[h] = total[h:h + 1, :]
        kt.append(jnp.transpose(head(k_ref, h)))
        weighted = kt[h].astype(F32) * tail_row[h:h + 1, :]
        local = dot_fine_left(weighted, head(v_ref, h))
        snd1[pl.ds(16 * h, 16)] = local.reshape(16, 8, D)

    pl.semaphore_wait(barrier, N_SEQ - 1 + N_DP - 1)
    for p in peers:
        send(dec_snd.at[lax.div(p, 16)], dec.at[me], 1, {"seq": p})
    dec[me] = dec_snd[lax.div(me, 16)]
    exchange(snd1, rcv1, 0)

    for h in range(H):
        qh = head(q_ref, h)
        qt[h] = jnp.transpose(qh)
        w = jnp.where(
            lower,
            jnp.exp(jnp.minimum(cum_col[:, h:h + 1] - cum_row[h:h + 1, :], 0.0)),
            0.0,
        )
        weights[h] = w
        m = (dot(qh, kt[h]) * w).astype(BF16)
        mixed[h] = m
        attn[h] = dot(m, head(v_ref, h))

    arrived(dec, N_SEQ - 1, 1)
    arrived(rcv1, N_SEQ - 1, 0)
    state = jnp.zeros((8, D), F32)
    for c in range(N_SEQ):
        out1[c] = state
        state = dec[c] * state + rcv1[c]
    exchange(out1, inc, 2)
    arrived(inc, N_SEQ - 1, 2)

    def state_of(buffer, h):
        return buffer[pl.ds(16 * h, 16)].reshape(D, D)

    square = jnp.zeros((T, D), F32)
    cross = jnp.zeros((T, D), F32)
    for h in range(H):
        outer = dot_fine_right(head(q_ref, h), state_of(inc, h)) * lead_col[:, h:h + 1]
        a = attn[h] + outer
        attn[h] = a
        scaled = head(g_ref, h).astype(F32) * gain_ref[:, h * D:(h + 1) * D]
        square = square + a * a
        cross = cross + scaled * a
    square = jnp.sum(square, axis=1, keepdims=True)
    cross = jnp.sum(cross, axis=1, keepdims=True)
    both = jnp.where(col_i == 0, square, jnp.where(col_i == 1, cross, 0.0))
    stat_snd[...] = jnp.transpose(both)[0:8, :]
    for p in partners:
        send(stat_snd, stat.at[mine], 3, {"dp": p})
    stat[mine] = stat_snd[...]
    arrived(stat, N_DP - 1, 3)
    sums = stat[0]
    for c in range(1, N_DP):
        sums = sums + stat[c]
    sums = jnp.transpose(jnp.concatenate([sums] * 16, axis=0)) * (1.0 / (N_DP * H * D))
    gz_snd[...] = jnp.zeros_like(gz_snd)
    inv = lax.rsqrt(sums[:, 0:1] + EPS)
    cross_mean = inv * sums[:, 1:2]

    for h in range(H):
        g = head(g_ref, h).astype(F32)
        scaled = g * gain_ref[:, h * D:(h + 1) * D]
        normed = attn[h] * inv
        d = (inv * (scaled - normed * cross_mean)).astype(BF16)
        d_attn[h] = d
        gz_snd[h:h + 1, :] = jnp.sum(g * normed, axis=0, keepdims=True)
        weighted = qt[h].astype(F32) * lead_row[h:h + 1, :]
        snd2[pl.ds(16 * h, 16)] = dot_fine_left(weighted, d).reshape(16, 8, D)
    exchange(snd2, rcv2, 4)
    for k in range(1, SIDE):
        send(gz_snd, gz.at[z], 5, {"seq": rows[0] + cols[k]})
    gz[z] = gz_snd[...]

    for h in range(H):
        qh, kh, vh, d = head(q_ref, h), head(k_ref, h), head(v_ref, h), d_attn[h]
        graded = (dot(d, vh, 1, 1) * weights[h]).astype(BF16)
        far = dot_fine_right(d, state_of(inc, h), 1, 1) * lead_col[:, h:h + 1]
        dq_ref[:, h * D:(h + 1) * D] = (dot(graded, kh) + far).astype(BF16)
        kg[h] = dot(graded, qh, 0, 0)
        vg[h] = dot(mixed[h], d, 0, 0)

    arrived(rcv2, N_SEQ - 1, 4)
    state = jnp.zeros((8, D), F32)
    for c in reversed(range(N_SEQ)):
        out2[c] = state
        state = dec[c] * state + rcv2[c]
    exchange(out2, lat, 6)
    arrived(gz, SIDE - 1, 5)
    part = gz[0]
    for c in range(1, SIDE):
        part = part + gz[c]
    gy_snd[...] = part
    for k in range(1, SIDE):
        send(gy_snd, gy.at[y], 7, {"seq": rows[k] + cols[0]})
    gy[y] = gy_snd[...]

    arrived(lat, N_SEQ - 1, 6)
    for h in range(H):
        kh, vh, tail = head(k_ref, h), head(v_ref, h), tail_col[:, h:h + 1]
        late = state_of(lat, h)
        dk_ref[:, h * D:(h + 1) * D] = (kg[h] + dot_fine_right(vh, late, 1, 1) * tail).astype(BF16)
        dv_ref[:, h * D:(h + 1) * D] = (vg[h] + dot_fine_right(kh, late) * tail).astype(BF16)
    arrived(gy, SIDE - 1, 7)
    part = gy[0]
    for c in range(1, SIDE):
        part = part + gy[c]
    dg_ref[...] = part[0:H, :]

    for buffer, count, at in (
        (rcv1, N_SEQ - 1, 0), (dec, N_SEQ - 1, 1), (inc, N_SEQ - 1, 2), (stat, N_DP - 1, 3),
        (rcv2, N_SEQ - 1, 4), (gz, SIDE - 1, 5), (lat, N_SEQ - 1, 6), (gy, SIDE - 1, 7),
    ):
        arrived(buffer, count, at, send_sems)


def on_device(queries, keys, values, output_gradient, log_decay, gain):
    vmem = pl.BlockSpec(memory_space=pltpu.VMEM)
    wide = jax.ShapeDtypeStruct((T, H * D), BF16)
    tiles = pltpu.VMEM((N_SEQ, 8, D), F32)
    dq, dk, dv, dg = pl.pallas_call(
        kernel,
        out_shape=(wide, wide, wide, jax.ShapeDtypeStruct((H, D), F32)),
        in_specs=[vmem] * 6,
        out_specs=(vmem,) * 4,
        scratch_shapes=[
            tiles, tiles, tiles, tiles, tiles, tiles, tiles, tiles,
            pltpu.VMEM((H, 1, D), F32),
            pltpu.VMEM((N_SEQ, 1, D), F32),
            pltpu.VMEM((8, T), F32),
            pltpu.VMEM((N_DP, 8, T), F32),
            pltpu.VMEM((8, D), F32),
            pltpu.VMEM((SIDE, 8, D), F32),
            pltpu.VMEM((8, D), F32),
            pltpu.VMEM((SIDE, 8, D), F32),
            pltpu.VMEM((H, D, T), BF16),
            pltpu.VMEM((H, T, T), F32),
            pltpu.VMEM((H, T, T), BF16),
            pltpu.VMEM((H, T, D), F32),
            pltpu.VMEM((H, T, D), BF16),
            pltpu.VMEM((H, T, D), F32),
            pltpu.VMEM((H, T, D), F32),
            pltpu.SemaphoreType.DMA((8,)),
            pltpu.SemaphoreType.DMA((8,)),
        ],
        compiler_params=pltpu.CompilerParams(
            collective_id=0, has_side_effects=True, vmem_limit_bytes=32 * 2**20
        ),
    )(queries, keys, values, output_gradient, log_decay, gain.reshape(1, H * D))
    return dq, dk, dv, dg.reshape(H * D)


def solution(mesh):
    return jax.shard_map(
        on_device,
        mesh=mesh,
        in_specs=(
            P("seq", "dp"),
            P("seq", "dp"),
            P("seq", "dp"),
            P("seq", "dp"),
            P("dp", "seq"),
            P("dp"),
        ),
        out_specs=(P("seq", "dp"), P("seq", "dp"), P("seq", "dp"), P("dp")),
        check_vma=False,
    )
```

time: 542 us -> 76 us (0.14)
  blocking collectives: 296 us -> 0 us
  other arithmetic: 143 us -> 0 us
  Pallas kernels: 0 us -> 67.6 us
  waiting for transfers between devices: 54.1 us -> 0 us
  local copies, waits for them, and re-layouts: 23 us -> 7.52 us
  between operations: 14.9 us -> 0.66 us
    psum x3 -> x0, blocking collectives: 165 us -> none  [the longest x1 115 us: on_device(): gain_grad = lax.psum(gain_part, 'seq')]
    select_n x126 -> x0, other arithmetic: 140 us -> none  [turn(): jnp.where(position < mine, new, old)]
    unnamed x1 -> x0, blocking collectives: 131 us -> none
    pallas_call x0 -> x1, Pallas kernels: none -> 67.6 us  [on_device(): pl.pallas_call(kernel, out_shape=(wide, wide, wide, jax.ShapeDtypeStruct(...]
    all_gather x2 -> x0, waiting for transfers between devices: 54.1 us -> none  [entering(): pieces = jax.tree.map(lambda part: lax.all_gather(part, axis), value)]
    rev x2 -> x0, local copies, waits for them, and re-layouts: 13.8 us -> none  [entering(): pieces = jax.tree.map(lambda part: part[::-1], pieces)]
  transfers between devices with their start and end apart: 2 -> 0, of which waited for: 2 -> 0; matrix products, arithmetic and copies ran while one was open for 1% -> 0% of each run, Pallas kernels for 0% -> 0%
where the time goes in v1:
time: 76 us; the launch traced here: 75.8 us
  Pallas kernels  67.6 us (89%)
  local copies, waits for them, and re-layouts  7.52 us (10%)
    pallas_call x1, Pallas kernels, on_device(): pl.pallas_call(kernel, out_shape=(wide, wide, wide, jax.ShapeDtypeStruct(...  67.6 us
    unnamed x16, local copies, waits for them, and re-layouts  7.52 us

profile of v1, /device:TPU:1, one launch (start us, length us, event | category | flops | bytes accessed | tf_op | source)
XLA Modules:
  0.0 75.8 jit_solution(15133141320679691061)
XLA Ops:
  0.6 0.0 copy-start
  0.6 0.9 %copy-done = bf16[128,512]{1,0:T(8,128)(2,1)S(1)} copy-done((bf16[128,512]{1,0:T(8,128)(2,1)S(1)}, bf16[128,512]{1,0:T(8,128)(2,1)}, u32[]{:S(2)}) %copy-start) | copy-done | bytes 131096
  1.5 0.0 copy-start.1
  1.5 0.9 %copy-done.1 = bf16[128,512]{1,0:T(8,128)(2,1)S(1)} copy-done((bf16[128,512]{1,0:T(8,128)(2,1)S(1)}, bf16[128,512]{1,0:T(8,128)(2,1)}, u32[]{:S(2)}) %copy-start.1) | copy-done | bytes 131096
  2.4 0.0 copy-start.2
  2.4 0.9 %copy-done.2 = bf16[128,512]{1,0:T(8,128)(2,1)S(1)} copy-done((bf16[128,512]{1,0:T(8,128)(2,1)S(1)}, bf16[128,512]{1,0:T(8,128)(2,1)}, u32[]{:S(2)}) %copy-start.2) | copy-done | bytes 131096
  3.3 0.0 copy-start.3
  3.3 0.9 %copy-done.3 = bf16[128,512]{1,0:T(8,128)(2,1)S(1)} copy-done((bf16[128,512]{1,0:T(8,128)(2,1)S(1)}, bf16[128,512]{1,0:T(8,128)(2,1)}, u32[]{:S(2)}) %copy-start.3) | copy-done | bytes 131096
  4.3 0.0 copy-start.4
  4.3 0.7 copy-done.4
  4.9 0.0 copy-start.5
  4.9 0.7 copy-done.5
  5.6 67.6 %shard_map.93 = (bf16[128,512]{1,0:T(8,128)(2,1)S(1)}, bf16[128,512]{1,0:T(8,128)(2,1)S(1)}, bf16[128,512]{1,0:T(8,128)(2,1)S(1)}, f32[4,128]{1,0:T(4,128)S(1)}) custom-call(bf16[128,512]{1,0:T(8,128)(2,1)S(1)} %copy-done, bf16[128,512]{1,0:T(8,128)(2,1)S(1)} %copy-done.1, bf16[128,512]{1,0:T(8,128)(2,1)S(1)} %copy-done.2, bf16[128,512]{1,0:T(8,128)(2,1)S(1)} %copy-done.3, ...), custom_call_target="tpu_custom_call" | custom-call | tf_op jit(solution)/shard_map/pallas_call | solution.py:227
  73.2 0.7 copy.14
  73.9 0.7 copy.15
  74.5 0.7 copy.16
  75.2 0.6 copy.17
Async XLA Ops:
  0.6 0.9 %copy-start = (bf16[128,512]{1,0:T(8,128)(2,1)S(1)}, bf16[128,512]{1,0:T(8,128)(2,1)}, u32[]{:S(2)}) copy-start(bf16[128,512]{1,0:T(8,128)(2,1)} %q_ref.1) | copy-start | bytes 393220
  1.5 0.9 %copy-start.1 = (bf16[128,512]{1,0:T(8,128)(2,1)S(1)}, bf16[128,512]{1,0:T(8,128)(2,1)}, u32[]{:S(2)}) copy-start(bf16[128,512]{1,0:T(8,128)(2,1)} %k_ref.1) | copy-start | bytes 393220
  2.4 0.9 %copy-start.2 = (bf16[128,512]{1,0:T(8,128)(2,1)S(1)}, bf16[128,512]{1,0:T(8,128)(2,1)}, u32[]{:S(2)}) copy-start(bf16[128,512]{1,0:T(8,128)(2,1)} %v_ref.1) | copy-start | bytes 393220
  3.3 0.9 %copy-start.3 = (bf16[128,512]{1,0:T(8,128)(2,1)S(1)}, bf16[128,512]{1,0:T(8,128)(2,1)}, u32[]{:S(2)}) copy-start(bf16[128,512]{1,0:T(8,128)(2,1)} %g_ref.1) | copy-start | bytes 393220
  4.3 0.7 copy-start.4
  4.9 0.7 copy-start.5

commit v2 on v1

--- a/solution.py
+++ b/solution.py
@@ -37,24 +37,44 @@
     return hi, (x - hi.astype(F32)).astype(BF16)
 
 
-def dot_fine_left(a, b, ca=1, cb=0):
-    hi, lo = split(a)
-    return dot(hi, b, ca, cb) + dot(lo, b, ca, cb)
-
-
-def dot_fine_right(a, b, ca=1, cb=0):
-    hi, lo = split(b)
-    return dot(a, hi, ca, cb) + dot(a, lo, ca, cb)
+def split_wide(x):
+    return jnp.concatenate(split(x), axis=1)
+
+
+def twice(x, axis):
+    return jnp.concatenate([x, x], axis=axis)
+
+
+def dot_fine_left(a, b):
+    return dot(split_wide(a), twice(b, 0))
+
+
+def dot_fine_right(a, b):
+    return dot(twice(a, 1), jnp.concatenate(split(b), axis=0))
+
+
+def dot_fine_right_t(a, b):
+    return dot(twice(a, 1), split_wide(b), 1, 1)
 
 
 def kernel(
-    q_ref, k_ref, v_ref, g_ref, ld_ref, gain_ref,
-    dq_ref, dk_ref, dv_ref, dg_ref,
-    snd1, rcv1, out1, inc, snd2, rcv2, out2, lat, dec_snd, dec,
+    q_hbm, k_hbm, v_hbm, g_hbm, ld_hbm, gain_hbm,
+    dq_ref, k_ref, v_ref, kg, vg, tail_ref, lat, dg_ref,
+    q_ref, g_ref, ld_ref, gain_ref,
+    snd1, rcv1, out1, inc, snd2, rcv2, out2, dec_snd, dec,
     stat_snd, stat, gz_snd, gz, gy_snd, gy,
-    qt, weights, mixed, attn, d_attn, kg, vg,
-    send_sems, recv_sems,
+    qt, weights, mixed, attn, d_attn,
+    send_sems, recv_sems, load_sems,
 ):
+    loads = [
+        pltpu.make_async_copy(src, dst, load_sems.at[i])
+        for i, (src, dst) in enumerate((
+            (ld_hbm, ld_ref), (k_hbm, k_ref), (v_hbm, v_ref),
+            (q_hbm, q_ref), (g_hbm, g_ref), (gain_hbm, gain_ref),
+        ))
+    ]
+    for load in loads:
+        load.start()
     me = lax.axis_index("seq")
     mine = lax.axis_index("dp")
     y, z = lax.div(me, SIDE), lax.rem(me, SIDE)
@@ -87,6 +107,7 @@
     row_i = lax.broadcasted_iota(jnp.int32, (T, T), 0)
     col_i = lax.broadcasted_iota(jnp.int32, (T, T), 1)
     lower = row_i >= col_i
+    loads[0].wait()
     log_decay = ld_ref[...]
     cum_row = dot(log_decay, jnp.where(row_i <= col_i, 1.0, 0.0), precision=HIGHEST)
     cum_col = dot(jnp.where(lower, 1.0, 0.0), log_decay, 1, 1, precision=HIGHEST)
@@ -101,6 +122,8 @@
         return ref[:, h * D:(h + 1) * D]
 
     kt = []
+    loads[1].wait()
+    loads[2].wait()
     for h in range(H):
         dec_snd[h] = total[h:h + 1, :]
         kt.append(jnp.transpose(head(k_ref, h)))
@@ -114,9 +137,12 @@
     dec[me] = dec_snd[lax.div(me, 16)]
     exchange(snd1, rcv1, 0)
 
+    for load in loads[3:]:
+        load.wait()
+    tail_ref[...] = tail_col
     for h in range(H):
         qh = head(q_ref, h)
-        qt[h] = jnp.transpose(qh)
+        qt[h] = split_wide(jnp.transpose(qh).astype(F32) * lead_row[h:h + 1, :])
         w = jnp.where(
             lower,
             jnp.exp(jnp.minimum(cum_col[:, h:h + 1] - cum_row[h:h + 1, :], 0.0)),
@@ -170,10 +196,11 @@
         normed = attn[h] * inv
         d = (inv * (scaled - normed * cross_mean)).astype(BF16)
         d_attn[h] = d
-        gz_snd[h:h + 1, :] = jnp.sum(g * normed, axis=0, keepdims=True)
-        weighted = qt[h].astype(F32) * lead_row[h:h + 1, :]
-        snd2[pl.ds(16 * h, 16)] = dot_fine_left(weighted, d).reshape(16, 8, D)
+        snd2[pl.ds(16 * h, 16)] = dot(qt[h], twice(d, 0)).reshape(16, 8, D)
     exchange(snd2, rcv2, 4)
+    for h in range(H):
+        normed = attn[h] * inv
+        gz_snd[h:h + 1, :] = jnp.sum(head(g_ref, h).astype(F32) * normed, axis=0, keepdims=True)
     for k in range(1, SIDE):
         send(gz_snd, gz.at[z], 5, {"seq": rows[0] + cols[k]})
     gz[z] = gz_snd[...]
@@ -181,7 +208,7 @@
     for h in range(H):
         qh, kh, vh, d = head(q_ref, h), head(k_ref, h), head(v_ref, h), d_attn[h]
         graded = (dot(d, vh, 1, 1) * weights[h]).astype(BF16)
-        far = dot_fine_right(d, state_of(inc, h), 1, 1) * lead_col[:, h:h + 1]
+        far = dot_fine_right_t(d, state_of(inc, h)) * lead_col[:, h:h + 1]
         dq_ref[:, h * D:(h + 1) * D] = (dot(graded, kh) + far).astype(BF16)
         kg[h] = dot(graded, qh, 0, 0)
         vg[h] = dot(mixed[h], d, 0, 0)
@@ -201,17 +228,12 @@
         send(gy_snd, gy.at[y], 7, {"seq": rows[k] + cols[0]})
     gy[y] = gy_snd[...]
 
-    arrived(lat, N_SEQ - 1, 6)
-    for h in range(H):
-        kh, vh, tail = head(k_ref, h), head(v_ref, h), tail_col[:, h:h + 1]
-        late = state_of(lat, h)
-        dk_ref[:, h * D:(h + 1) * D] = (kg[h] + dot_fine_right(vh, late, 1, 1) * tail).astype(BF16)
-        dv_ref[:, h * D:(h + 1) * D] = (vg[h] + dot_fine_right(kh, late) * tail).astype(BF16)
     arrived(gy, SIDE - 1, 7)
     part = gy[0]
     for c in range(1, SIDE):
         part = part + gy[c]
     dg_ref[...] = part[0:H, :]
+    arrived(lat, N_SEQ - 1, 6)
 
     for buffer, count, at in (
         (rcv1, N_SEQ - 1, 0), (dec, N_SEQ - 1, 1), (inc, N_SEQ - 1, 2), (stat, N_DP - 1, 3),
@@ -220,17 +242,61 @@
         arrived(buffer, count, at, send_sems)
 
 
+def finish(
+    dq_ref, k_ref, v_ref, kg, vg, tail_ref, lat, dg_ref,
+    dq_out, dk_out, dv_out, dg_out, dk_ref, dv_ref, sems,
+):
+    def start(src, dst, at):
+        copy = pltpu.make_async_copy(src, dst, sems.at[at])
+        copy.start()
+        return copy
+
+    copies = [start(dq_ref, dq_out, 0), start(dg_ref, dg_out, 1)]
+    for h in range(H):
+        part = pl.ds(h * D, D)
+        late = lat[pl.ds(16 * h, 16)].reshape(D, D)
+        far = dot_fine_right_t(v_ref[:, part], late)
+        dk_ref[:, part] = (kg[h] + far * tail_ref[:, h:h + 1]).astype(BF16)
+    copies.append(start(dk_ref, dk_out, 2))
+    for h in range(H):
+        part = pl.ds(h * D, D)
+        late = lat[pl.ds(16 * h, 16)].reshape(D, D)
+        far = dot_fine_right(k_ref[:, part], late)
+        dv_ref[:, part] = (vg[h] + far * tail_ref[:, h:h + 1]).astype(BF16)
+    copies.append(start(dv_ref, dv_out, 3))
+    for copy in copies:
+        copy.wait()
+
+
 def on_device(queries, keys, values, output_gradient, log_decay, gain):
     vmem = pl.BlockSpec(memory_space=pltpu.VMEM)
-    wide = jax.ShapeDtypeStruct((T, H * D), BF16)
+    hbm = pl.BlockSpec(memory_space=pltpu.HBM)
+    flat = (T, H * D)
+    wide = jax.ShapeDtypeStruct(flat, BF16)
+    small = jax.ShapeDtypeStruct((H, D), F32)
     tiles = pltpu.VMEM((N_SEQ, 8, D), F32)
-    dq, dk, dv, dg = pl.pallas_call(
+    inside = [
+        pltpu.VMEM(s, t)
+        for s, t in (
+            (flat, BF16), (flat, BF16), (flat, BF16), ((H, T, D), F32), ((H, T, D), F32),
+            ((T, H), F32), ((N_SEQ, 8, D), F32), ((H, D), F32),
+        )
+    ]
+    inputs = [
+        pltpu.with_memory_space_constraint(x, pltpu.HBM)
+        for x in (queries, keys, values, output_gradient, log_decay, gain.reshape(1, H * D))
+    ]
+    middle = pl.pallas_call(
         kernel,
-        out_shape=(wide, wide, wide, jax.ShapeDtypeStruct((H, D), F32)),
-        in_specs=[vmem] * 6,
-        out_specs=(vmem,) * 4,
+        out_shape=inside,
+        in_specs=[hbm] * 6,
+        out_specs=(vmem,) * 8,
         scratch_shapes=[
-            tiles, tiles, tiles, tiles, tiles, tiles, tiles, tiles,
+            pltpu.VMEM(flat, BF16),
+            pltpu.VMEM(flat, BF16),
+            pltpu.VMEM((H, T), F32),
+            pltpu.VMEM((1, H * D), F32),
+            tiles, tiles, tiles, tiles, tiles, tiles, tiles,
             pltpu.VMEM((H, 1, D), F32),
             pltpu.VMEM((N_SEQ, 1, D), F32),
             pltpu.VMEM((8, T), F32),
@@ -239,20 +305,32 @@
             pltpu.VMEM((SIDE, 8, D), F32),
             pltpu.VMEM((8, D), F32),
             pltpu.VMEM((SIDE, 8, D), F32),
-            pltpu.VMEM((H, D, T), BF16),
+            pltpu.VMEM((H, D, 2 * T), BF16),
             pltpu.VMEM((H, T, T), F32),
             pltpu.VMEM((H, T, T), BF16),
             pltpu.VMEM((H, T, D), F32),
             pltpu.VMEM((H, T, D), BF16),
-            pltpu.VMEM((H, T, D), F32),
-            pltpu.VMEM((H, T, D), F32),
             pltpu.SemaphoreType.DMA((8,)),
             pltpu.SemaphoreType.DMA((8,)),
+            pltpu.SemaphoreType.DMA((6,)),
         ],
         compiler_params=pltpu.CompilerParams(
             collective_id=0, has_side_effects=True, vmem_limit_bytes=32 * 2**20
         ),
-    )(queries, keys, values, output_gradient, log_decay, gain.reshape(1, H * D))
+    )(*inputs)
+    middle = [pltpu.with_memory_space_constraint(x, pltpu.VMEM) for x in middle]
+    dq, dk, dv, dg = pl.pallas_call(
+        finish,
+        out_shape=(wide, wide, wide, small),
+        in_specs=[vmem] * 8,
+        out_specs=(hbm,) * 4,
+        scratch_shapes=[
+            pltpu.VMEM(flat, BF16),
+            pltpu.VMEM(flat, BF16),
+            pltpu.SemaphoreType.DMA((4,)),
+        ],
+        compiler_params=pltpu.CompilerParams(vmem_limit_bytes=16 * 2**20),
+    )(*middle)
     return dq, dk, dv, dg.reshape(H * D)
 
 

time: 76 us -> 68.7 us (0.904)
  local copies, waits for them, and re-layouts: 7.52 us -> 0 us
    unnamed x16 -> x0, local copies, waits for them, and re-layouts: 7.52 us -> none
    pallas_call x1 -> x2, Pallas kernels: 67.6 us -> 67.9 us  [the longest x1 66.9 us: on_device(): pl.pallas_call(kernel, out_shape=inside, in_specs=[hbm] * 6, out_specs=(v...]
where the time goes in v2:
time: 68.7 us; the launch traced here: 68.6 us
  Pallas kernels  67.9 us (99%)
    pallas_call x1, Pallas kernels, on_device(): pl.pallas_call(kernel, out_shape=inside, in_specs=[hbm] * 6, out_specs=(v...  66.9 us

profile of v2, /device:TPU:1, one launch (start us, length us, event | category | flops | bytes accessed | tf_op | source)
XLA Modules:
  0.0 68.6 jit_solution(13691122364002614469)
XLA Ops:
  0.6 66.9 %shard_map.93 = (bf16[128,512]{1,0:T(8,128)(2,1)S(1)}, bf16[128,512]{1,0:T(8,128)(2,1)S(1)}, bf16[128,512]{1,0:T(8,128)(2,1)S(1)}, f32[4,128,128]{2,1,0:T(8,128)...) custom-call(bf16[128,512]{1,0:T(8,128)(2,1)} %q_hbm.1, ...), custom_call_target="tpu_custom_call" | custom-call | tf_op jit(solution)/shard_map/pallas_call | solution.py:289
  67.5 1.0 %shard_map.94 = (bf16[128,512]{1,0:T(8,128)(2,1)}, bf16[128,512]{1,0:T(8,128)(2,1)}, bf16[128,512]{1,0:T(8,128)(2,1)}, f32[4,128]{1,0:T(4,128)}) custom-call(bf16[128,512]{1,0:T(8,128)(2,1)S(1)} %get-tuple-element.16.dq_ref, bf16[128,512]{1,0:T(8,128)(2,1)S(1)} %get-tuple-element.17.k_ref, bf16[128,512]{1,0:T(8,128)(2,1)S(1)} %get-tuple-element.18.v_ref, ...), custom_call_target="tpu_custom_call" | custom-call | tf_op jit(solution)/shard_map/pallas_call | solution.py:322
